TPU v7x, 32 devices: a whole 2x2x4 slice. The times are simulated.
32 devices in a mesh: dp: 8 (over z, y), head: 4 (over x, core).
Axes of the slice: x: 2, y: 2, z: 4, core: 2. Of those that a mesh axis runs over, the one named last changes fastest.
Arguments:
- block_input_rows: bfloat16 [32, 1024, 1024], P('dp', 'head'), may hold values from -6 to 6
- document_starts: int32 [32, 1024], P('dp'), may hold values from 0 to 1023, as said below
- counted_mask: int32 [32, 1024], P('dp', 'head'), may hold values from 0 to 1
- output_gradient: bfloat16 [32, 1024, 1024], P('dp', 'head'), may hold values from -6 to 6
- first_norm_gain: bfloat16 [1024], replicated, may hold values from 0.099609375 to 1.8984375
- first_norm_bias: bfloat16 [1024], replicated, may hold values from -4 to 4
- query_key_value_weight: bfloat16 [1024, 3072], replicated, may hold values from -0.1875 to 0.1875
- query_down_weight: bfloat16 [1024, 4], replicated, may hold values from -0.1875 to 0.1875
- query_up_weight: bfloat16 [4, 1024], replicated, may hold values from -0.75 to 0.75
- value_down_weight: bfloat16 [1024, 4], replicated, may hold values from -0.1875 to 0.1875
- value_up_weight: bfloat16 [4, 1024], replicated, may hold values from -0.75 to 0.75
- attention_out_weight: bfloat16 [1024, 1024], replicated, may hold values from -0.75 to 0.75
- second_norm_gain: bfloat16 [1024], replicated, may hold values from 0.099609375 to 1.8984375
- second_norm_bias: bfloat16 [1024], replicated, may hold values from -4 to 4
- feed_input_weight: bfloat16 [1024, 4096], replicated, may hold values from -0.1875 to 0.1875
- feed_input_bias: bfloat16 [4096], replicated, may hold values from -6 to 6
- feed_output_weight: bfloat16 [4096, 1024], replicated, may hold values from -0.09375 to 0.09375
Outputs:
- output: bfloat16 [32, 1024, 1024], P('dp', 'head')
- input_grad: bfloat16 [32, 1024, 1024], P('dp', 'head')
- grad_lora_aq: float32 [1024, 4], replicated
- grad_lora_bq: float32 [4, 1024], replicated
- grad_lora_av: float32 [1024, 4], replicated
- grad_lora_bv: float32 [4, 1024], replicated
- rms_values: float32 [2], replicated
Inputs may be any that keep to these rules, and one draw needn't show every extreme that they name: `document_starts`: within each slot a token's id is the position of the first token of its document, so ids never fall along the slot. In each aligned group of 4 slots one slot, drawn from the seed, is a single document; in every other slot the last token is a document of its own.
All inputs are finite; a program needn't handle non-finite values.
Results may differ from a plain program's by a relative error of at most 0.013.
Values may be sent and summed in bfloat16 or wider, within the bound.
A program may use at most 192 MiB of HBM per device.

v0:
```python
import jax
import jax.numpy as jnp
from jax import lax
from jax.sharding import PartitionSpec as P

H = 16


EPSILON = 1e-05
ADAPTER_SCALE = 8.0
NEGATIVE = -1e30


def as_sent(x):

    def short(part):
        return part.astype(jnp.bfloat16) if part.dtype == jnp.float32 else part

    return jax.tree.map(short, x)


def norm_rows(matrix, gain_vec, shift_vec):
    center = matrix - jnp.mean(matrix, axis=-1, keepdims=True)
    variance = jnp.mean(center * center, axis=-1, keepdims=True)
    return center * lax.rsqrt(variance + EPSILON) * gain_vec + shift_vec


def norm_back(matrix, gain_vec, shift_vec, incoming):
    pullback = jax.vjp(lambda element_item: norm_rows(element_item, gain_vec, shift_vec), matrix)[1]
    return pullback(incoming)[0]


def gelu_tanh(matrix):
    return jax.nn.gelu(matrix, approximate=True)


def plain_product(left, right):
    return jnp.dot(left, right, preferred_element_type=jnp.float32)


def last_product(left, right):
    return lax.dot_general(
        left, right, (((1,), (1,)), ((), ())), preferred_element_type=jnp.float32
    )


def first_product(left, right):
    return lax.dot_general(
        left, right, (((0,), (0,)), ((), ())), preferred_element_type=jnp.float32
    )


def masked_scores(query_block, key_slot, segments, row_start, row_end, score_scale):
    places = jnp.arange(row_end)
    allowed = (segments[row_start:row_end, None] == segments[None, :row_end]) & (
        places[None, :] <= places[row_start:row_end, None]
    )
    scores = (
        jnp.einsum(
            "qhd,khd->hqk", query_block, key_slot[:row_end], preferred_element_type=jnp.float32
        )
        * score_scale
    )
    return jnp.where(allowed[None], scores, NEGATIVE)


def attend_slot(query_slot, key_slot, value_slot, segments, block_rows, score_scale):
    length = query_slot.shape[0]
    outputs_list = []
    logsum_list = []
    for block_index in range(length // block_rows):
        row_start = block_index * block_rows
        row_end = row_start + block_rows
        scores = masked_scores(
            query_slot[row_start:row_end], key_slot, segments, row_start, row_end, score_scale
        )
        row_max = jnp.max(scores, axis=-1, keepdims=True)
        exponent = jnp.exp(scores - row_max)
        row_total = jnp.sum(exponent, axis=-1, keepdims=True)
        probability = (exponent / row_total).astype(jnp.bfloat16)
        context = jnp.einsum(
            "hqk,khd->qhd", probability, value_slot[:row_end], preferred_element_type=jnp.float32
        )
        outputs_list.append(context.astype(jnp.bfloat16))
        logsum_list.append((row_max + jnp.log(row_total))[..., 0])
    return (jnp.concatenate(outputs_list, 0), jnp.concatenate(logsum_list, 1))


def attend_back(
    query_slot, key_slot, value_slot, grad_slot, logsum, segments, block_rows, score_scale
):
    length = query_slot.shape[0]
    key_grad = jnp.zeros(key_slot.shape, jnp.float32)
    value_gradient = jnp.zeros(value_slot.shape, jnp.float32)
    query_parts = []
    for block_index in range(length // block_rows):
        row_start = block_index * block_rows
        row_end = row_start + block_rows
        query_block = query_slot[row_start:row_end]
        grad_block = grad_slot[row_start:row_end]
        scores = masked_scores(query_block, key_slot, segments, row_start, row_end, score_scale)
        probability = jnp.exp(scores - logsum[:, row_start:row_end, None])
        prob_grad = jnp.einsum(
            "qhd,khd->hqk", grad_block, value_slot[:row_end], preferred_element_type=jnp.float32
        )
        inner_sum = jnp.sum(probability * prob_grad, axis=-1, keepdims=True)
        score_grad = (probability * (prob_grad - inner_sum)).astype(jnp.bfloat16)
        query_parts.append(
            jnp.einsum(
                "hqk,khd->qhd", score_grad, key_slot[:row_end], preferred_element_type=jnp.float32
            )
            * score_scale
        )
        key_grad = key_grad.at[:row_end].add(
            jnp.einsum("hqk,qhd->khd", score_grad, query_block, preferred_element_type=jnp.float32)
            * score_scale
        )
        value_gradient = value_gradient.at[:row_end].add(
            jnp.einsum(
                "hqk,qhd->khd",
                probability.astype(jnp.bfloat16),
                grad_block,
                preferred_element_type=jnp.float32,
            )
        )
    query_gradient = jnp.concatenate(query_parts, 0)
    return (
        query_gradient.astype(jnp.bfloat16),
        key_grad.astype(jnp.bfloat16),
        value_gradient.astype(jnp.bfloat16),
    )


def shards(
    block_input_rows,
    document_starts,
    counted_mask,
    output_gradient,
    first_norm_gain,
    first_norm_bias,
    query_key_value_weight,
    query_down_weight,
    query_up_weight,
    value_down_weight,
    value_up_weight,
    attention_out_weight,
    second_norm_gain,
    second_norm_bias,
    feed_input_weight,
    feed_input_bias,
    feed_output_weight,
):
    slot_count, local_len, row_width = block_input_rows.shape
    groups = lax.axis_size("head")
    full_len = local_len * groups
    head_size = row_width // H
    heads_here = H // groups
    row_count = slot_count * local_len
    block_rows = min(512, full_len)
    score_scale = head_size ** (-0.5)
    gain_one = first_norm_gain.astype(jnp.float32)
    shift_one = first_norm_bias.astype(jnp.float32)
    gain_two = second_norm_gain.astype(jnp.float32)
    shift_two = second_norm_bias.astype(jnp.float32)
    fc_bias = feed_input_bias.astype(jnp.float32)
    local_shape = (slot_count, local_len, row_width)
    split_shape = (slot_count, full_len, heads_here, head_size)
    merged_shape = (slot_count, full_len, heads_here * head_size)
    flat_in = block_input_rows.reshape(row_count, row_width).astype(jnp.float32)
    normed_rows = norm_rows(flat_in, gain_one, shift_one).astype(jnp.bfloat16)
    query_low_rank = plain_product(normed_rows, query_down_weight).astype(jnp.bfloat16)
    value_low_rank = plain_product(normed_rows, value_down_weight).astype(jnp.bfloat16)
    projected_rows = plain_product(normed_rows, query_key_value_weight)
    query_rows = (
        projected_rows[:, :row_width]
        + ADAPTER_SCALE * plain_product(query_low_rank, query_up_weight)
    ).astype(jnp.bfloat16)
    key_rows = projected_rows[:, row_width : 2 * row_width].astype(jnp.bfloat16)
    value_matrix = (
        projected_rows[:, 2 * row_width :]
        + ADAPTER_SCALE * plain_product(value_low_rank, value_up_weight)
    ).astype(jnp.bfloat16)
    head_query, head_key, head_value = (
        lax.all_to_all(
            query_rows.reshape(local_shape), "head", split_axis=2, concat_axis=1, tiled=True
        ),
        lax.all_to_all(
            key_rows.reshape(local_shape), "head", split_axis=2, concat_axis=1, tiled=True
        ),
        lax.all_to_all(
            value_matrix.reshape(local_shape), "head", split_axis=2, concat_axis=1, tiled=True
        ),
    )
    head_query = head_query.reshape(split_shape)
    head_key = head_key.reshape(split_shape)
    head_value = head_value.reshape(split_shape)

    def slot_fn(packed):
        return attend_slot(packed[0], packed[1], packed[2], packed[3], block_rows, score_scale)

    context_heads, logsum = lax.map(slot_fn, (head_query, head_key, head_value, document_starts))
    context_local = lax.all_to_all(
        as_sent(context_heads.reshape(merged_shape)),
        "head",
        split_axis=1,
        concat_axis=2,
        tiled=True,
    )
    context_flat = context_local.reshape(row_count, row_width)
    branch = plain_product(context_flat, attention_out_weight)
    hidden_state = flat_in + branch
    normed_two = norm_rows(hidden_state, gain_two, shift_two).astype(jnp.bfloat16)
    before = plain_product(normed_two, feed_input_weight) + fc_bias
    activated = gelu_tanh(before).astype(jnp.bfloat16)
    feed_out = plain_product(activated, feed_output_weight)
    result = hidden_state + feed_out
    output = result.astype(jnp.bfloat16).reshape(block_input_rows.shape)
    valid_rows = counted_mask.reshape(row_count).astype(jnp.float32)[:, None]
    square_sums = jnp.stack(
        [
            jnp.sum(valid_rows * result * result),
            jnp.sum(valid_rows * (branch * branch + feed_out * feed_out)),
            jnp.sum(valid_rows),
        ]
    )
    grad_flat = output_gradient.reshape(row_count, row_width)
    act_grad = last_product(grad_flat, feed_output_weight)
    gelu_pull = jax.vjp(gelu_tanh, before)[1]
    before_grad = gelu_pull(act_grad)[0].astype(jnp.bfloat16)
    normed_two_grad = last_product(before_grad, feed_input_weight)
    hidden_grad = grad_flat.astype(jnp.float32) + norm_back(
        hidden_state, gain_two, shift_two, normed_two_grad
    )
    branch_grad = hidden_grad.astype(jnp.bfloat16)
    context_grad = last_product(branch_grad, attention_out_weight).astype(jnp.bfloat16)
    grad_heads = lax.all_to_all(
        context_grad.reshape(local_shape), "head", split_axis=2, concat_axis=1, tiled=True
    ).reshape(split_shape)

    def back_fn(packed):
        return attend_back(
            packed[0],
            packed[1],
            packed[2],
            packed[3],
            packed[4],
            packed[5],
            block_rows,
            score_scale,
        )

    query_gradient, key_grad, value_gradient = lax.map(
        back_fn, (head_query, head_key, head_value, grad_heads, logsum, document_starts)
    )
    query_gradient, key_grad, value_gradient = (
        lax.all_to_all(
            as_sent(query_gradient.reshape(merged_shape)),
            "head",
            split_axis=1,
            concat_axis=2,
            tiled=True,
        ),
        lax.all_to_all(
            as_sent(key_grad.reshape(merged_shape)), "head", split_axis=1, concat_axis=2, tiled=True
        ),
        lax.all_to_all(
            as_sent(value_gradient.reshape(merged_shape)),
            "head",
            split_axis=1,
            concat_axis=2,
            tiled=True,
        ),
    )
    query_gradient = query_gradient.reshape(row_count, row_width)
    key_grad = key_grad.reshape(row_count, row_width)
    value_gradient = value_gradient.reshape(row_count, row_width)
    query_low_gradient = (ADAPTER_SCALE * last_product(query_gradient, query_up_weight)).astype(
        jnp.bfloat16
    )
    value_low_gradient = (ADAPTER_SCALE * last_product(value_gradient, value_up_weight)).astype(
        jnp.bfloat16
    )
    joined_grads = jnp.concatenate([query_gradient, key_grad, value_gradient], axis=1)
    normed_grad = (
        last_product(joined_grads, query_key_value_weight)
        + last_product(query_low_gradient, query_down_weight)
        + last_product(value_low_gradient, value_down_weight)
    )
    input_grad = hidden_grad + norm_back(flat_in, gain_one, shift_one, normed_grad)
    down_query = first_product(normed_rows, query_low_gradient)
    lifted_query = ADAPTER_SCALE * first_product(query_low_rank, query_gradient)
    down_value = first_product(normed_rows, value_low_gradient)
    lifted_value = ADAPTER_SCALE * first_product(value_low_rank, value_gradient)
    totals = lax.psum(
        (down_query, lifted_query, down_value, lifted_value, square_sums), ("dp", "head")
    )
    token_count = jnp.maximum(totals[4][2], 1.0)
    rms_values = jnp.stack(
        [
            jnp.sqrt(totals[4][0] / (token_count * row_width)),
            jnp.sqrt(totals[4][1] / (2.0 * token_count * row_width)),
        ]
    )
    return (
        output,
        input_grad.astype(jnp.bfloat16).reshape(block_input_rows.shape),
        totals[0],
        totals[1],
        totals[2],
        totals[3],
        rms_values,
    )


def solution(mesh):
    return jax.shard_map(
        shards,
        mesh=mesh,
        in_specs=(
            P("dp", "head", None),
            P("dp", None),
            P("dp", "head"),
            P("dp", "head", None),
            P(),
            P(),
            P(),
            P(),
            P(),
            P(),
            P(),
            P(),
            P(),
            P(),
            P(),
            P(),
            P(),
        ),
        out_specs=(P("dp", "head", None), P("dp", "head", None), P(), P(), P(), P(), P()),
        check_vma=False,
    )
```

profile of v0, /device:TPU:0, one launch (start us, length us, event | category | flops | bytes accessed | tf_op | source)
XLA Modules:
  0.0 739.9 jit_solution(6997054266342214226)
XLA Ops:
  15.6 6.7 fusion.152
  31.7 4.6 all-to-all-start.2
  47.7 15.0 %all-to-all-done.2 = bf16[4,256,1024]{1,0,2:T(4,128)(2,1)} async-done(((bf16[4,256,1024]{1,0,2:T(4,128)(2,1)}), bf16[4,256,1024]{1,0,2:T(4,128)(2,1)}, u32[]{:S(2)}, u32[]{:S(2)}) %all-to-all-start.2) | async-done | bytes 2097184 | tf_op jit(solution)/shard_map/all_to_all | solution.py:187
  62.6 4.5 all-to-all-start.1
  78.5 14.4 %all-to-all-done.1 = bf16[4,256,1024]{1,0,2:T(4,128)(2,1)} async-done(((bf16[4,256,1024]{1,0,2:T(4,128)(2,1)}), bf16[4,256,1024]{1,0,2:T(4,128)(2,1)}, u32[]{:S(2)}, u32[]{:S(2)}) %all-to-all-start.1) | async-done | bytes 2097184 | tf_op jit(solution)/shard_map/all_to_all | solution.py:184
  92.9 4.6 all-to-all-start
  97.5 4.5 copy.81
  102.0 4.5 reshape.610
  106.5 4.5 copy.79
  111.0 4.5 reshape.608
  115.5 7.7 %all-to-all-done = bf16[4,256,1024]{1,0,2:T(4,128)(2,1)} async-done(((bf16[4,256,1024]{1,0,2:T(4,128)(2,1)}), bf16[4,256,1024]{1,0,2:T(4,128)(2,1)}, u32[]{:S(2)}, u32[]{:S(2)}) %all-to-all-start) | async-done | bytes 2097184 | tf_op jit(solution)/shard_map/all_to_all | solution.py:190
  123.2 4.5 copy.77
  133.8 65.7 %while.35 = (s32[]{:T(128)}, bf16[4,1024,4,64]{1,3,2,0:T(8,128)(2,1)}, f32[4,4,1024]{2,1,0:T(4,128)}, bf16[4,1024,4,64]{1,3,2,0:T(8,128)(2,1)}, s32[4,1024]{1,0:...) while((s32[]{:T(128)}, ...), condition=%wide.region_7.8_spmd, body=%wide.region_2.7_spmd.sunk | while | flops 846725120 | bytes 44765844 | solution.py:201
  203.8 4.8 all-to-all-start.3
  208.6 25.6 %all-to-all-done.3 = bf16[4,1024,256]{2,0,1:T(4,128)(2,1)} async-done(((bf16[4,1024,256]{2,0,1:T(4,128)(2,1)}), bf16[4,1024,256]{2,0,1:T(4,128)(2,1)}, u32[]{:S(2)}, u32[]{:S(2)}) %all-to-all-start.3) | async-done | bytes 2097184 | tf_op jit(solution)/shard_map/all_to_all | solution.py:202
  243.3 12.6 %fusion.121 = f32[1024,4096]{1,0:T(8,128)} fusion(bf16[1024,4096]{1,0:T(8,128)(2,1)S(1)} %bitcast.382, f32[1024,1024]{1,0:T(8,128)S(1)} %get-tuple-element.325, f32[1024]{0:T(1024)S(1)} %convert_element_type.165, f32[1024]{0:T(1024)S(1)} %convert_element_type.164, f32[1024]{0:T(1024)S(1)} %fusion.132, f32[1024]{0:T(1024)S(1)} %broadcast_multiply_fusion), kind=kOutput, calls=%fused_computation.165 | convolution fusion | flops 8595177472 | bytes 29376512 | tf_op jit(solution)/shard_map/dot_general | solution.py:38
  255.9 41.3 %fusion.98 = f32[1024,1024]{1,0:T(8,128)} fusion(bf16[1024,4096]{1,0:T(8,128)(2,1)} %param.47, f32[1024,4096]{1,0:T(8,128)} %fusion.121, f32[4096]{0:T(1024)S(1)} %convert_element_type.167, bf16[1024,1024]{1,0:T(8,128)(2,1)} %bitcast.362, bf16[4096,1024]{1,0:T(8,128)(2,1)} %param.49), kind=kOutput, calls=%fused_computation.127 | convolution fusion | flops 17267949568 | bytes 39862272 | tf_op jit(solution)/shard_map/dot_general | solution.py:42
  297.2 22.3 %fusion.106 = (f32[]{:T(128)}, f32[]{:T(128)}, f32[1024]{0:T(1024)S(1)}, bf16[1024,1024]{1,0:T(8,128)(2,1)}) fusion(f32[1024]{0:T(1024)S(1)} %bitcast.380, f32[1024,1024]{1,0:T(8,128)} %copy-done.14, f32[1024,1024]{1,0:T(8,128)} %get-tuple-element.348, f32[1024,1024]{1,0:T(8,128)} %fusion.98, f32[1024]{0:T(1024)S(1)} %convert_element_type.164, ...), kind=kOutput, calls=%fused_computation.137 | convolution fusion | flops 8646556672 | bytes 39878664 | tf_op jit(solution)/shard_map/dot_general | solution.py:38
  331.2 4.5 all-to-all-start.4
  335.6 25.8 %all-to-all-done.4 = bf16[4,256,1024]{1,0,2:T(4,128)(2,1)} async-done(((bf16[4,256,1024]{1,0,2:T(4,128)(2,1)}), bf16[4,256,1024]{1,0,2:T(4,128)(2,1)}, u32[]{:S(2)}, u32[]{:S(2)}) %all-to-all-start.4) | async-done | bytes 2097184 | tf_op jit(solution)/shard_map/all_to_all | solution.py:236
  361.4 4.5 copy.86
  365.9 4.5 reshape.616
  375.3 112.7 %while.36 = (s32[]{:T(128)}, bf16[4,1024,4,64]{1,3,2,0:T(8,128)(2,1)}, bf16[4,1024,4,64]{1,3,2,0:T(8,128)(2,1)}, bf16[4,1024,4,64]{1,3,2,0:T(8,128)(2,1)}, bf16[...) while((s32[]{:T(128)}, ...), condition=%wide.region_15.16_spmd, body=%wide.region_12.15_spmd.sunk | while | flops 2065821696 | bytes 123660512 | solution.py:252
  492.2 4.5 all-to-all-start.5
  501.0 21.5 %all-to-all-done.5 = bf16[4,1024,256]{2,0,1:T(4,128)(2,1)} async-done(((bf16[4,1024,256]{2,0,1:T(4,128)(2,1)}), bf16[4,1024,256]{2,0,1:T(4,128)(2,1)}, u32[]{:S(2)}, u32[]{:S(2)}) %all-to-all-start.5) | async-done | bytes 2097184 | tf_op jit(solution)/shard_map/all_to_all | solution.py:256
  522.5 4.5 all-to-all-start.7
  540.4 12.2 %all-to-all-done.7 = bf16[4,1024,256]{2,0,1:T(4,128)(2,1)} async-done(((bf16[4,1024,256]{2,0,1:T(4,128)(2,1)}), bf16[4,1024,256]{2,0,1:T(4,128)(2,1)}, u32[]{:S(2)}, u32[]{:S(2)}) %all-to-all-start.7) | async-done | bytes 2097184 | tf_op jit(solution)/shard_map/all_to_all | solution.py:266
  552.7 4.5 all-to-all-start.6
  569.3 13.6 %all-to-all-done.6 = bf16[4,1024,256]{2,0,1:T(4,128)(2,1)} async-done(((bf16[4,1024,256]{2,0,1:T(4,128)(2,1)}), bf16[4,1024,256]{2,0,1:T(4,128)(2,1)}, u32[]{:S(2)}, u32[]{:S(2)}) %all-to-all-start.6) | async-done | bytes 2097184 | tf_op jit(solution)/shard_map/all_to_all | solution.py:263
  588.4 10.6 %fusion.100 = f32[1024,1024]{1,0:T(8,128)S(1)} fusion(bf16[1024,3072]{1,0:T(8,128)(2,1)} %param.39, bf16[1024,1024]{1,0:T(8,128)(2,1)S(1)} %bitcast.347, bf16[1024,1024]{1,0:T(8,128)(2,1)} %bitcast.366, bf16[1024,1024]{1,0:T(8,128)(2,1)S(1)} %bitcast.344), kind=kOutput, calls=%fused_computation.128 | convolution fusion | flops 6461325312 | bytes 16777216 | tf_op jit(solution)/shard_map/dot_general | solution.py:42
  602.6 6.6 add_convert_fusion
  609.1 114.5 %all-reduce.5.cloned.1.call-done = (f32[1024,4]{0,1:T(4,128)}, f32[4,1024]{1,0:T(4,128)}, f32[1024,4]{0,1:T(4,128)}, f32[4,1024]{1,0:T(4,128)}, f32[3]{0:T(128)}) async-done(((f32[1024,4]{0,1:T(4,128)}, f32[4,1024]{1,0:T(4,128)}, f32[1024,4]{0,1:T(4,128)}, f32[4,1024]{1,0:T(4,128)}, f32[3]{0:T(128)}), (f32[1024,4]{0,1:T(4,128)}, f32[4,1024]{1,0:T(4,128)}, f32[1024,4]{0,1:T(4,128)}, f32[4,1024]{1,0:T(4,128)}, ...) | async-done | bytes 65564 | tf_op jit(solution)/shard_map/psum | solution.py:294
  (336 shorter events, 303.2 us)
Async XLA Ops:
  7.2 231.1 %copy-start = (bf16[1024,1024]{1,0:T(8,128)(2,1)S(1)}, bf16[1024,1024]{1,0:T(8,128)(2,1)}, u32[]{:S(2)}) copy-start(bf16[1024,1024]{1,0:T(8,128)(2,1)} %param.44) | copy-start | bytes 6291460
  7.2 7.6 %copy-start.2 = (bf16[4,256,1024]{2,1,0:T(8,128)(2,1)S(1)}, bf16[4,256,1024]{2,1,0:T(8,128)(2,1)}, u32[]{:S(2)}) copy-start(bf16[4,256,1024]{2,1,0:T(8,128)(2,1)} %param.33) | copy-start | bytes 6291460
  8.0 6.1 copy-start.32
  8.8 6.7 copy-start.49
  15.6 6.7 copy-start.5
  22.3 5.1 copy-start.18
  27.4 8.9 %copy-start.38 = (bf16[1024,4]{0,1:T(4,128)(2,1)S(1)}, bf16[1024,4]{0,1:T(4,128)(2,1)}, u32[]{:S(2)}) copy-start(bf16[1024,4]{0,1:T(4,128)(2,1)} %param.40) | copy-start | bytes 24580
  31.7 7.5 %copy-start.34 = (bf16[4,1024]{1,0:T(4,128)(2,1)S(1)}, bf16[4,1024]{1,0:T(4,128)(2,1)}, u32[]{:S(2)}) copy-start(bf16[4,1024]{1,0:T(4,128)(2,1)} %param.41) | copy-start | bytes 24580
  31.7 31.0 %all-to-all-start.2 = ((bf16[4,256,1024]{1,0,2:T(4,128)(2,1)}), bf16[4,256,1024]{1,0,2:T(4,128)(2,1)}, u32[]{:S(2)}, u32[]{:S(2)}) async-start(bf16[4,256,1024]{1,0,2:T(4,128)(2,1)} %copy.80), calls=%async_computation.2 | async-start | bytes 4194304 | tf_op jit(solution)/shard_map/all_to_all | solution.py:187
  43.4 23.7 %copy-start.40 = (bf16[1024,4]{0,1:T(4,128)(2,1)S(1)}, bf16[1024,4]{0,1:T(4,128)(2,1)}, u32[]{:S(2)}) copy-start(bf16[1024,4]{0,1:T(4,128)(2,1)} %param.42) | copy-start | bytes 24580
  47.7 22.3 %copy-start.36 = (bf16[4,1024]{1,0:T(4,128)(2,1)S(1)}, bf16[4,1024]{1,0:T(4,128)(2,1)}, u32[]{:S(2)}) copy-start(bf16[4,1024]{1,0:T(4,128)(2,1)} %param.43) | copy-start | bytes 24580
  62.6 30.2 %all-to-all-start.1 = ((bf16[4,256,1024]{1,0,2:T(4,128)(2,1)}), bf16[4,256,1024]{1,0,2:T(4,128)(2,1)}, u32[]{:S(2)}, u32[]{:S(2)}) async-start(bf16[4,256,1024]{1,0,2:T(4,128)(2,1)} %copy.78), calls=%async_computation.1 | async-start | bytes 4194304 | tf_op jit(solution)/shard_map/all_to_all | solution.py:184
  92.9 30.4 %all-to-all-start = ((bf16[4,256,1024]{1,0,2:T(4,128)(2,1)}), bf16[4,256,1024]{1,0,2:T(4,128)(2,1)}, u32[]{:S(2)}, u32[]{:S(2)}) async-start(bf16[4,256,1024]{1,0,2:T(4,128)(2,1)} %copy.76), calls=%async_computation | async-start | bytes 4194304 | tf_op jit(solution)/shard_map/all_to_all | solution.py:190
  127.8 6.0 copy-start.20
  199.5 9.1 %copy-start.47 = (bf16[1024]{0:T(1024)(128)(2,1)S(1)}, bf16[1024]{0:T(1024)(128)(2,1)}, u32[]{:S(2)}) copy-start(bf16[1024]{0:T(1024)(128)(2,1)} %param.45) | copy-start | bytes 6148
  199.5 9.1 %copy-start.48 = (bf16[1024]{0:T(1024)(128)(2,1)S(1)}, bf16[1024]{0:T(1024)(128)(2,1)}, u32[]{:S(2)}) copy-start(bf16[1024]{0:T(1024)(128)(2,1)} %param.46) | copy-start | bytes 6148
  199.5 9.1 %copy-start.44 = (s32[4,256]{1,0:T(4,128)S(1)}, s32[4,256]{1,0:T(4,128)}, u32[]{:S(2)}) copy-start(s32[4,256]{1,0:T(4,128)} %param.35) | copy-start | bytes 12292
  199.5 9.1 %copy-start.46 = (bf16[4096]{0:T(1024)(128)(2,1)S(1)}, bf16[4096]{0:T(1024)(128)(2,1)}, u32[]{:S(2)}) copy-start(bf16[4096]{0:T(1024)(128)(2,1)} %param.48) | copy-start | bytes 24580
  203.8 30.5 %all-to-all-start.3 = ((bf16[4,1024,256]{2,0,1:T(4,128)(2,1)}), bf16[4,1024,256]{2,0,1:T(4,128)(2,1)}, u32[]{:S(2)}, u32[]{:S(2)}) async-start(bf16[4,1024,256]{2,0,1:T(4,128)(2,1)} %copy.82), calls=%async_computation.3 | async-start | bytes 4194304 | tf_op jit(solution)/shard_map/all_to_all | solution.py:202
  242.7 13.2 %copy-start.14 = (f32[1024,1024]{1,0:T(8,128)}, f32[1024,1024]{1,0:T(8,128)S(1)}, u32[]{:S(2)}) copy-start(f32[1024,1024]{1,0:T(8,128)S(1)} %get-tuple-element.325) | copy-start | bytes 12582916
  297.2 22.3 %copy-start.15 = (f32[1024,1024]{1,0:T(8,128)S(1)}, f32[1024,1024]{1,0:T(8,128)}, u32[]{:S(2)}) copy-start(f32[1024,1024]{1,0:T(8,128)} %copy-done.14) | copy-start | bytes 12582916
  331.2 30.2 %all-to-all-start.4 = ((bf16[4,256,1024]{1,0,2:T(4,128)(2,1)}), bf16[4,256,1024]{1,0,2:T(4,128)(2,1)}, u32[]{:S(2)}, u32[]{:S(2)}) async-start(bf16[4,256,1024]{1,0,2:T(4,128)(2,1)} %copy.85), calls=%async_computation.4 | async-start | bytes 4194304 | tf_op jit(solution)/shard_map/all_to_all | solution.py:236
  492.2 30.2 %all-to-all-start.5 = ((bf16[4,1024,256]{2,0,1:T(4,128)(2,1)}), bf16[4,1024,256]{2,0,1:T(4,128)(2,1)}, u32[]{:S(2)}, u32[]{:S(2)}) async-start(bf16[4,1024,256]{2,0,1:T(4,128)(2,1)} %copy.87), calls=%async_computation.5 | async-start | bytes 4194304 | tf_op jit(solution)/shard_map/all_to_all | solution.py:256
  496.7 30.2 %copy-start.45 = (s32[4,256]{1,0:T(4,128)S(1)}, s32[4,256]{1,0:T(4,128)}, u32[]{:S(2)}) copy-start(s32[4,256]{1,0:T(4,128)} %param.35) | copy-start | bytes 12292
  522.5 30.2 %all-to-all-start.7 = ((bf16[4,1024,256]{2,0,1:T(4,128)(2,1)}), bf16[4,1024,256]{2,0,1:T(4,128)(2,1)}, u32[]{:S(2)}, u32[]{:S(2)}) async-start(bf16[4,1024,256]{2,0,1:T(4,128)(2,1)} %copy.93), calls=%async_computation.7 | async-start | bytes 4194304 | tf_op jit(solution)/shard_map/all_to_all | solution.py:266
  552.7 30.2 %all-to-all-start.6 = ((bf16[4,1024,256]{2,0,1:T(4,128)(2,1)}), bf16[4,1024,256]{2,0,1:T(4,128)(2,1)}, u32[]{:S(2)}, u32[]{:S(2)}) async-start(bf16[4,1024,256]{2,0,1:T(4,128)(2,1)} %copy.90), calls=%async_computation.6 | async-start | bytes 4194304 | tf_op jit(solution)/shard_map/all_to_all | solution.py:263
  557.2 166.5 %all-reduce.5.cloned.1.call-start = ((), (), s32[]{:S(2)}) async-start(), calls=%async_computation.8 | async-start | bytes 132096 | tf_op jit(solution)/shard_map/psum | solution.py:294
  588.3 10.6 %copy-start.4 = (bf16[4,256,1024]{2,1,0:T(8,128)(2,1)S(1)}, bf16[4,256,1024]{2,1,0:T(8,128)(2,1)}, u32[]{:S(2)}) copy-start(bf16[4,256,1024]{2,1,0:T(8,128)(2,1)} %param.33) | copy-start | bytes 6291460
  588.3 10.6 %copy-start.16 = (f32[1024,1024]{1,0:T(8,128)S(1)}, f32[1024,1024]{1,0:T(8,128)}, u32[]{:S(2)}) copy-start(f32[1024,1024]{1,0:T(8,128)} %fusion.153) | copy-start | bytes 12582916
  588.3 10.6 %copy-start.23 = (f32[1,2,4,128]{3,1,2,0:T(2,128)S(1)}, f32[1,2,4,128]{3,1,2,0:T(2,128)}, u32[]{:S(2)}) copy-start(f32[1,2,4,128]{3,1,2,0:T(2,128)} %copy-done.22) | copy-start | bytes 12292
  588.3 10.6 %copy-start.33 = (f32[1024]{0:T(1024)S(1)}, f32[1024]{0:T(1024)}, u32[]{:S(2)}) copy-start(f32[1024]{0:T(1024)} %copy-done.32) | copy-start | bytes 12292
  588.3 10.6 %copy-start.41 = (bf16[1024,4]{0,1:T(4,128)(2,1)S(1)}, bf16[1024,4]{0,1:T(4,128)(2,1)}, u32[]{:S(2)}) copy-start(bf16[1024,4]{0,1:T(4,128)(2,1)} %param.42) | copy-start | bytes 24580
  (35 other events, 93.7 us)
Sparse Core Ops, SparseCore 0:
  602.7 120.8 all-reduce.4
where the time goes:
time: 752 us; the launch traced here: 740 us
  matrix products  253 us (34%)
  waiting for transfers between devices  250 us (33%)
  local copies, waits for them, and re-layouts  116 us (15%)
  other arithmetic  66.4 us (9%)
  starting transfers between devices  36.3 us (5%)
  between operations  17 us (2%)
    psum x1, waiting for transfers between devices, shards(): lax.psum((down_query, lifted_query, down_value, lifted_value, square_sums...  114 us
    dot_general x7, matrix products, last_product(): lax.dot_general(left, right, (((1,), (1,)), ((), ())), preferred_element_...  61.3 us
    dot_general x8, matrix products, plain_product(): return jnp.dot(left, right, preferred_element_type=jnp.float32)  59 us
    dot_general x16, matrix products, masked_scores(): jnp.einsum('qhd,khd->hqk', query_block, key_slot[:row_end], preferred_ele...  35.2 us
    dot_general x8, matrix products, attend_back(): jnp.einsum('qhd,khd->hqk', grad_block, value_slot[:row_end], preferred_el...  26.7 us
    all_to_all x1, waiting for transfers between devices, shards(): lax.all_to_all(context_grad.reshape(local_shape), 'head', split_axis=2, c...  25.8 us
    all_to_all x1, waiting for transfers between devices, shards(): lax.all_to_all(as_sent(context_heads.reshape(merged_shape)), 'head', spli...  25.6 us
    dot_general x8, matrix products, attend_slot(): jnp.einsum('hqk,khd->qhd', probability, value_slot[:row_end], preferred_e...  23.7 us
  transfers between devices with their start and end apart: 9, of which 9 were waited for; matrix products, arithmetic and copies ran while one was open for 10% of the time, Pallas kernels for 0%

commit v1 on v0

--- a/solution.py
+++ b/solution.py
@@ -1,6 +1,10 @@
+import functools
+
 import jax
 import jax.numpy as jnp
 from jax import lax
+from jax.experimental import pallas as pl
+from jax.experimental.pallas import tpu as pltpu
 from jax.sharding import PartitionSpec as P
 
 H = 16
@@ -312,9 +316,618 @@
     )
 
 
+LOG2E = 1.4426950408889634
+LN2 = 0.6931471805599453
+TILE = 256
+GROUP = 256
+bf16 = jnp.bfloat16
+f32 = jnp.float32
+NT = (((1,), (1,)), ((), ()))
+NN = (((1,), (0,)), ((), ()))
+TN = (((0,), (0,)), ((), ()))
+MESH = pl.DeviceIdType.MESH
+MIB = 2**20
+
+
+def dg(left, right, dims):
+    return lax.dot_general(left, right, dims, preferred_element_type=f32)
+
+
+def resident(shape):
+    zeros = (0,) * len(shape)
+    return pl.BlockSpec(shape, lambda *_: zeros, pipeline_mode=pl.Buffered(1))
+
+
+def params(mib):
+    return pltpu.CompilerParams(
+        vmem_limit_bytes=mib * MIB, dimension_semantics=("arbitrary",)
+    )
+
+
+def norm_stats(rows):
+    center = rows - jnp.mean(rows, axis=-1, keepdims=True)
+    rs = lax.rsqrt(jnp.mean(center * center, axis=-1, keepdims=True) + EPSILON)
+    return center * rs, rs
+
+
+def norm_grad(unit, rs, gain, incoming):
+    t = incoming * gain
+    return (
+        t - jnp.mean(t, axis=-1, keepdims=True) - unit * jnp.mean(t * unit, axis=-1, keepdims=True)
+    ) * rs
+
+
+def qkv_kernel(x_ref, gain_ref, shift_ref, w_ref, down_ref, upq_ref, upv_ref, qkv_ref, normed_ref, low_ref):
+    width = x_ref.shape[-1]
+    unit, _ = norm_stats(x_ref[0].astype(f32))
+    normed = (unit * gain_ref[...] + shift_ref[...]).astype(bf16)
+    normed_ref[...] = normed
+    low = dg(normed, down_ref[...], NN).astype(bf16)
+    low_ref[...] = low
+    head_size = width // H
+    scale = head_size**-0.5 * LOG2E
+    step = 512
+    for at in range(0, width, step):
+        part = dg(normed, w_ref[:, at : at + step], NN)
+        part = part + ADAPTER_SCALE * dg(low, upq_ref[:, at : at + step], NN)
+        qkv_ref[:, at : at + step] = (part * scale).astype(bf16)
+    for at in range(width, 2 * width, step):
+        qkv_ref[:, at : at + step] = dg(normed, w_ref[:, at : at + step], NN).astype(bf16)
+    for at in range(0, width, step):
+        part = dg(normed, w_ref[:, 2 * width + at : 2 * width + at + step], NN)
+        part = part + ADAPTER_SCALE * dg(low, upv_ref[:, at : at + step], NN)
+        qkv_ref[:, 2 * width + at : 2 * width + at + step] = part.astype(bf16)
+
+
+def project(x, gain, shift, w, down, upq, upv):
+    blocks, tile, width = x.shape
+    rows = blocks * tile
+    ranks = down.shape[1]
+    return pl.pallas_call(
+        qkv_kernel,
+        grid=(blocks,),
+        in_specs=[
+            pl.BlockSpec((1, tile, width), lambda i: (i, 0, 0)),
+            resident((1, width)),
+            resident((1, width)),
+            resident(w.shape),
+            resident(down.shape),
+            resident(upq.shape),
+            resident(upv.shape),
+        ],
+        out_specs=[
+            pl.BlockSpec((tile, 3 * width), lambda i: (i, 0)),
+            pl.BlockSpec((tile, width), lambda i: (i, 0)),
+            pl.BlockSpec((tile, ranks), lambda i: (i, 0)),
+        ],
+        out_shape=[
+            jax.ShapeDtypeStruct((rows, 3 * width), bf16),
+            jax.ShapeDtypeStruct((rows, width), bf16),
+            jax.ShapeDtypeStruct((rows, ranks), bf16),
+        ],
+        compiler_params=params(40),
+        cost_estimate=pl.CostEstimate(flops=2 * rows * width * 3 * width, bytes_accessed=20 * MIB, transcendentals=0),
+        name="project",
+    )(x, gain, shift, w, down, upq, upv)
+
+
+def head_masks(x, heads, size):
+    lane = lax.broadcasted_iota(jnp.int32, x.shape, 1)
+    return [
+        jnp.where((lane >= size * h) & (lane < size * (h + 1)), x, jnp.zeros_like(x))
+        for h in range(heads)
+    ]
+
+
+def merge_heads(stacked, heads, size):
+    rows = stacked.shape[0] // heads
+    out = stacked[:rows]
+    lane = lax.broadcasted_iota(jnp.int32, out.shape, 1)
+    for h in range(1, heads):
+        out = jnp.where(lane >= size * h, stacked[h * rows : (h + 1) * rows], out)
+    return out
+
+
+def attend_kernel(start_ref, q_ref, k_ref, v_ref, o_ref, p_ref, s_sc, bias_sc, *, size, strip):
+    length = q_ref.shape[0]
+    heads = q_ref.shape[1] // size
+    blocks = length // TILE
+
+    @pl.when(pl.program_id(0) == 0)
+    def _():
+        for i in range(blocks):
+            n = (i + 1) * TILE
+            for r in range(i * TILE, n, strip):
+                keys = lax.broadcasted_iota(jnp.int32, (strip, n), 1)
+                rows = lax.broadcasted_iota(jnp.int32, (strip, n), 0) + r
+                allowed = (keys >= start_ref[r : r + strip, :]) & (keys <= rows)
+                bias_sc[r : r + strip, 0:n] = jnp.where(allowed, 0.0, NEGATIVE)
+
+    def scores(i):
+        masked = jnp.concatenate(head_masks(q_ref[i * TILE : (i + 1) * TILE, :], heads, size), 0)
+        for j in range(i + 1):
+            s_sc[i % 2, :, j * TILE : (j + 1) * TILE] = dg(masked, k_ref[j * TILE : (j + 1) * TILE, :], NT)
+
+    def soft(i):
+        n = (i + 1) * TILE
+        for r in range(0, TILE, strip):
+            for h in range(heads):
+                at = h * TILE + r
+                s = s_sc[i % 2, at : at + strip, 0:n] + bias_sc[i * TILE + r : i * TILE + r + strip, 0:n]
+                e = jnp.exp2(s - jnp.max(s, axis=1, keepdims=True))
+                total = jnp.sum(e, axis=1, keepdims=True)
+                p_ref[h, i * TILE + r : i * TILE + r + strip, 0:n] = (e * (1.0 / total)).astype(bf16)
+
+    def mix(i):
+        n = (i + 1) * TILE
+        probs = p_ref[:, i * TILE : n, 0:n].reshape(heads * TILE, n)
+        o_ref[i * TILE : n, :] = merge_heads(dg(probs, v_ref[0:n, :], NN), heads, size).astype(bf16)
+
+    for t in range(blocks + 2):
+        if t < blocks:
+            scores(t)
+        if 0 <= t - 1 < blocks:
+            soft(t - 1)
+        if 0 <= t - 2 < blocks:
+            mix(t - 2)
+
+
+def attend(starts, qkv, size):
+    length, wide = qkv.shape
+    width = wide // 3
+    groups = width // GROUP
+    per = GROUP // size
+    return pl.pallas_call(
+        functools.partial(attend_kernel, size=size, strip=32),
+        grid=(groups,),
+        in_specs=[
+            resident((length, 1)),
+            pl.BlockSpec((length, GROUP), lambda g: (0, g)),
+            pl.BlockSpec((length, GROUP), lambda g: (0, g + groups)),
+            pl.BlockSpec((length, GROUP), lambda g: (0, g + 2 * groups)),
+        ],
+        out_specs=[
+            pl.BlockSpec((length, GROUP), lambda g: (0, g)),
+            pl.BlockSpec((per, length, length), lambda g: (g, 0, 0)),
+        ],
+        out_shape=[
+            jax.ShapeDtypeStruct((length, width), bf16),
+            jax.ShapeDtypeStruct((per * groups, length, length), bf16),
+        ],
+        scratch_shapes=[
+            pltpu.VMEM((2, per * TILE, length), f32),
+            pltpu.VMEM((length, length), f32),
+        ],
+        compiler_params=params(48),
+        cost_estimate=pl.CostEstimate(flops=20 * 10**9, bytes_accessed=40 * MIB, transcendentals=0),
+        name="attend",
+    )(starts, qkv, qkv, qkv)
+
+
+def attend_back_kernel(q_ref, k_ref, v_ref, g_ref, o_ref, p_ref, dq_ref, dk_ref, dv_ref, dp_sc, ds_sc, dk_sc, dv_sc, *, size, strip):
+    length = q_ref.shape[0]
+    heads = q_ref.shape[1] // size
+    blocks = length // TILE
+    scale = size**-0.5
+
+    def stack(ref, i):
+        return jnp.concatenate(head_masks(ref[i * TILE : (i + 1) * TILE, :], heads, size), 0)
+
+    def prob_grads(i):
+        masked = stack(g_ref, i)
+        for j in range(i + 1):
+            dp_sc[i % 2, :, j * TILE : (j + 1) * TILE] = dg(masked, v_ref[j * TILE : (j + 1) * TILE, :], NT)
+
+    def score_grads(i):
+        n = (i + 1) * TILE
+        both = g_ref[i * TILE : n, :].astype(f32) * o_ref[i * TILE : n, :].astype(f32)
+        for h in range(heads):
+            for r in range(0, TILE, strip):
+                at = h * TILE + r
+                inner = jnp.sum(both[r : r + strip, size * h : size * (h + 1)], axis=1, keepdims=True)
+                prob = p_ref[h, i * TILE + r : i * TILE + r + strip, 0:n].astype(f32)
+                ds_sc[i % 2, at : at + strip, 0:n] = (prob * (dp_sc[i % 2, at : at + strip, 0:n] - inner)).astype(bf16)
+
+    def products(i):
+        n = (i + 1) * TILE
+        dq = merge_heads(dg(ds_sc[i % 2, :, 0:n], k_ref[0:n, :], NN), heads, size)
+        dq_ref[i * TILE : n, :] = (dq * scale).astype(bf16)
+        grad4 = stack(g_ref, i)
+        query4 = stack(q_ref, i)
+        for j in range(i + 1):
+            at = slice(j * TILE, (j + 1) * TILE)
+            dv = dg(p_ref[:, i * TILE : n, at].reshape(heads * TILE, TILE), grad4, TN)
+            dk = dg(ds_sc[i % 2, :, at], query4, TN)
+            if i == j:
+                dv_sc[at] = dv
+                dk_sc[at] = dk
+            else:
+                dv_sc[at] += dv
+                dk_sc[at] += dk
+
+    for t in range(blocks + 2):
+        if t < blocks:
+            prob_grads(t)
+        if 0 <= t - 1 < blocks:
+            score_grads(t - 1)
+        if 0 <= t - 2 < blocks:
+            products(t - 2)
+    dk_ref[...] = (dk_sc[...] * LN2).astype(bf16)
+    dv_ref[...] = dv_sc[...].astype(bf16)
+
+
+def attend_back_slot(qkv, grad, context, probs, size):
+    length, wide = qkv.shape
+    width = wide // 3
+    groups = width // GROUP
+    per = GROUP // size
+    part = pl.BlockSpec((length, GROUP), lambda g: (0, g))
+    return pl.pallas_call(
+        functools.partial(attend_back_kernel, size=size, strip=32),
+        grid=(groups,),
+        in_specs=[
+            part,
+            pl.BlockSpec((length, GROUP), lambda g: (0, g + groups)),
+            pl.BlockSpec((length, GROUP), lambda g: (0, g + 2 * groups)),
+            part,
+            part,
+            pl.BlockSpec((per, length, length), lambda g: (g, 0, 0)),
+        ],
+        out_specs=[part] * 3,
+        out_shape=[jax.ShapeDtypeStruct((length, width), bf16)] * 3,
+        scratch_shapes=[
+            pltpu.VMEM((2, per * TILE, length), f32),
+            pltpu.VMEM((2, per * TILE, length), bf16),
+            pltpu.VMEM((length, GROUP), f32),
+            pltpu.VMEM((length, GROUP), f32),
+        ],
+        compiler_params=params(56),
+        cost_estimate=pl.CostEstimate(flops=30 * 10**9, bytes_accessed=45 * MIB, transcendentals=0),
+        name="attend_back",
+    )(qkv, qkv, qkv, grad, context, probs)
+
+
+def feed_kernel(
+    x_ref, y_ref, ctx_ref, mask_ref, wo_ref, gain_ref, shift_ref, wi_ref, bias_ref, wf_ref,
+    out_ref, hg_ref, cg_ref, sums_ref, fwd_sc, bwd_sc,
+):
+    width = x_ref.shape[-1]
+    hidden_units = wi_ref.shape[1]
+    branch = dg(ctx_ref[...], wo_ref[...], NN)
+    hidden = x_ref[0].astype(f32) + branch
+    unit, rs = norm_stats(hidden)
+    gain = gain_ref[...]
+    normed = (unit * gain + shift_ref[...]).astype(bf16)
+    dy = y_ref[0]
+    step = 512
+    c0 = 0.7978845608028654
+    c1 = c0 * 0.044715
+    for at in range(0, hidden_units, step):
+        v = dg(normed, wi_ref[:, at : at + step], NN) + bias_ref[:, at : at + step]
+        act_grad = dg(dy, wf_ref[at : at + step, :], NT)
+        square = v * v
+        half = 0.5 * jnp.tanh(v * (c0 + c1 * square)) + 0.5
+        act = v * half
+        slope = half + act * (1.0 - half) * (2.0 * c0 + 6.0 * c1 * square)
+        fwd_sc[:, at : at + step] = act.astype(bf16)
+        bwd_sc[:, at : at + step] = (slope * act_grad).astype(bf16)
+    feed = dg(fwd_sc[...], wf_ref[...], NN)
+    result = hidden + feed
+    out_ref[0] = result.astype(bf16)
+    valid = mask_ref[...]
+    one = jnp.sum(valid * (result * result))
+    two = jnp.sum(valid * (branch * branch + feed * feed))
+    count = jnp.sum(valid)
+    row = lax.broadcasted_iota(jnp.int32, sums_ref.shape, 0)
+    col = lax.broadcasted_iota(jnp.int32, sums_ref.shape, 1)
+    mine = jnp.where(col == 0, one, jnp.where(col == 1, two, jnp.where(col == 2, count, 0.0)))
+    mine = jnp.where(row == 0, mine, 0.0)
+
+    @pl.when(pl.program_id(0) == 0)
+    def _():
+        sums_ref[...] = mine
+
+    @pl.when(pl.program_id(0) > 0)
+    def _():
+        sums_ref[...] += mine
+
+    normed_grad = dg(bwd_sc[...], wi_ref[...], NT)
+    hidden_grad = dy.astype(f32) + norm_grad(unit, rs, gain, normed_grad)
+    low = hidden_grad.astype(bf16)
+    hg_ref[...] = low
+    cg_ref[...] = dg(low, wo_ref[...], NT).astype(bf16)
+
+
+def feed(x, dy, context, mask, wo, gain, shift, wi, bias, wf):
+    blocks, tile, width = x.shape
+    rows = blocks * tile
+    units = wi.shape[1]
+    slab = pl.BlockSpec((1, tile, width), lambda i: (i, 0, 0))
+    flat = pl.BlockSpec((tile, width), lambda i: (i, 0))
+    return pl.pallas_call(
+        feed_kernel,
+        grid=(blocks,),
+        in_specs=[
+            slab, slab, flat,
+            pl.BlockSpec((tile, 1), lambda i: (i, 0)),
+            resident(wo.shape), resident((1, width)), resident((1, width)),
+            resident(wi.shape), resident((1, units)), resident(wf.shape),
+        ],
+        out_specs=[slab, flat, flat, pl.BlockSpec((8, width), lambda i: (0, 0))],
+        out_shape=[
+            jax.ShapeDtypeStruct(x.shape, bf16),
+            jax.ShapeDtypeStruct((rows, width), bf16),
+            jax.ShapeDtypeStruct((rows, width), bf16),
+            jax.ShapeDtypeStruct((8, width), f32),
+        ],
+        scratch_shapes=[pltpu.VMEM((tile, units), bf16), pltpu.VMEM((tile, units), bf16)],
+        compiler_params=params(60),
+        cost_estimate=pl.CostEstimate(flops=2 * rows * width * (4 * units + 2 * width), bytes_accessed=30 * MIB, transcendentals=0),
+        name="feed",
+    )(x, dy, context, mask, wo, gain, shift, wi, bias, wf)
+
+
+def qkv_back_kernel(
+    x_ref, hg_ref, dq_ref, dk_ref, dv_ref, normed_ref, low_ref, gain_ref, w_ref, down_ref, upq_ref, upv_ref, sums_ref,
+    out_ref, grads_ref,
+):
+    width = x_ref.shape[-1]
+    ranks = down_ref.shape[1]
+    half = ranks // 2
+    dq, dk, dv = dq_ref[...], dk_ref[...], dv_ref[...]
+    low_grad = (ADAPTER_SCALE * (dg(dq, upq_ref[...], NT) + dg(dv, upv_ref[...], NT))).astype(bf16)
+    normed_grad = (
+        dg(dq, w_ref[:, :width], NT)
+        + dg(dk, w_ref[:, width : 2 * width], NT)
+        + dg(dv, w_ref[:, 2 * width :], NT)
+        + dg(low_grad, down_ref[...], NT)
+    )
+    unit, rs = norm_stats(x_ref[0].astype(f32))
+    out_ref[0] = (hg_ref[...].astype(f32) + norm_grad(unit, rs, gain_ref[...], normed_grad)).astype(bf16)
+    downs = dg(low_grad, normed_ref[...], TN)
+    low = low_ref[...]
+    ups_q = ADAPTER_SCALE * dg(low, dq, TN)[:half]
+    ups_v = ADAPTER_SCALE * dg(low, dv, TN)[half:]
+    mine = jnp.concatenate([downs, ups_q, ups_v], 0)
+
+    @pl.when(pl.program_id(0) == 0)
+    def _():
+        grads_ref[0 : 2 * ranks] = mine
+        grads_ref[2 * ranks :] = sums_ref[...]
+
+    @pl.when(pl.program_id(0) > 0)
+    def _():
+        grads_ref[0 : 2 * ranks] += mine
+
+
+def project_back(x, hidden_grad, dq, dk, dv, normed, low, gain, w, down, upq, upv, sums):
+    blocks, tile, width = x.shape
+    ranks = down.shape[1]
+    slab = pl.BlockSpec((1, tile, width), lambda i: (i, 0, 0))
+    flat = pl.BlockSpec((tile, width), lambda i: (i, 0))
+    return pl.pallas_call(
+        qkv_back_kernel,
+        grid=(blocks,),
+        in_specs=[
+            slab, flat, flat, flat, flat, flat,
+            pl.BlockSpec((tile, ranks), lambda i: (i, 0)),
+            resident((1, width)), resident(w.shape), resident(down.shape), resident(upq.shape), resident(upv.shape),
+            resident(sums.shape),
+        ],
+        out_specs=[slab, pl.BlockSpec((2 * ranks + 8, width), lambda i: (0, 0))],
+        out_shape=[
+            jax.ShapeDtypeStruct(x.shape, bf16),
+            jax.ShapeDtypeStruct((2 * ranks + 8, width), f32),
+        ],
+        compiler_params=params(40),
+        cost_estimate=pl.CostEstimate(flops=2 * blocks * tile * width * 3 * width, bytes_accessed=20 * MIB, transcendentals=0),
+        name="project_back",
+    )(x, hidden_grad, dq, dk, dv, normed, low, gain, w, down, upq, upv, sums)
+
+
+def swap_slabs(me, group, count, refs, send_sem, recv_sem, local_sem):
+    copies = []
+    for a, (src, dst) in enumerate(refs):
+        local = pltpu.make_async_copy(src.at[me], dst.at[me], local_sem.at[a])
+        local.start()
+        copies.append(local)
+    order = [k for k in range(count - 1, 0, -1)]
+    for a, (src, dst) in enumerate(refs):
+        for k in order:
+            peer = lax.rem(me + k, count)
+            copy = pltpu.make_async_remote_copy(
+                src_ref=src.at[peer],
+                dst_ref=dst.at[me],
+                send_sem=send_sem.at[a, k],
+                recv_sem=recv_sem.at[a, k],
+                device_id=(group, peer),
+                device_id_type=MESH,
+            )
+            copy.start()
+            copies.append(copy)
+    return copies
+
+
+def entry_barrier(peers):
+    barrier = pltpu.get_barrier_semaphore()
+    for peer in peers:
+        pl.semaphore_signal(barrier, inc=1, device_id=peer, device_id_type=MESH)
+    pl.semaphore_wait(barrier, len(peers))
+
+
+def arrive_kernel(x_ref, mask_ref, xs_ref, masks_ref, send_sem, recv_sem, local_sem):
+    count = x_ref.shape[0]
+    group, me = lax.axis_index("dp"), lax.axis_index("head")
+    entry_barrier([(group, lax.rem(me + k, count)) for k in range(1, count)])
+    for copy in swap_slabs(me, group, count, [(x_ref, xs_ref), (mask_ref, masks_ref)], send_sem, recv_sem, local_sem):
+        copy.wait()
+
+
+def arrive(x, mask):
+    count = x.shape[0]
+    anywhere = pl.BlockSpec(memory_space=pl.ANY)
+    return pl.pallas_call(
+        arrive_kernel,
+        in_specs=[anywhere] * 2,
+        out_specs=[anywhere] * 2,
+        out_shape=[jax.ShapeDtypeStruct(x.shape, x.dtype), jax.ShapeDtypeStruct(mask.shape, mask.dtype)],
+        scratch_shapes=[
+            pltpu.SemaphoreType.DMA((2, count)),
+            pltpu.SemaphoreType.DMA((2, count)),
+            pltpu.SemaphoreType.DMA((2,)),
+        ],
+        compiler_params=pltpu.CompilerParams(collective_id=0, has_side_effects=True),
+        name="arrive",
+    )(x, mask)
+
+
+def leave_kernel(x_ref, part_ref, xs_ref, total_ref, sums, heard, send_sem, recv_sem, local_sem, sum_send, sum_recv, *, sizes):
+    count = x_ref.shape[0]
+    group, me = lax.axis_index("dp"), lax.axis_index("head")
+    swaps = []
+    step = 1
+    while step < sizes[1]:
+        swaps.append((group, me ^ step))
+        step *= 2
+    step = 1
+    while step < sizes[0]:
+        swaps.append((group ^ step, me))
+        step *= 2
+    entry_barrier([(group, lax.rem(me + k, count)) for k in range(1, count)] + swaps[count.bit_length() - 1 :])
+    copies = swap_slabs(me, group, count, [(x_ref, xs_ref)], send_sem, recv_sem, local_sem)
+    sums[0] = part_ref[...]
+    for at, peer in enumerate(swaps):
+        copy = pltpu.make_async_remote_copy(
+            src_ref=sums.at[at],
+            dst_ref=heard.at[at],
+            send_sem=sum_send.at[at],
+            recv_sem=sum_recv.at[at],
+            device_id=peer,
+            device_id_type=MESH,
+        )
+        copy.start()
+        copy.wait()
+        if at + 1 < len(swaps):
+            sums[at + 1] = sums[at] + heard[at]
+        else:
+            total_ref[...] = sums[at] + heard[at]
+    for copy in copies:
+        copy.wait()
+
+
+def leave(x, part, sizes):
+    count = x.shape[0]
+    steps = (sizes[0].bit_length() - 1) + (sizes[1].bit_length() - 1)
+    anywhere = pl.BlockSpec(memory_space=pl.ANY)
+    inside = pl.BlockSpec(memory_space=pltpu.VMEM)
+    return pl.pallas_call(
+        functools.partial(leave_kernel, sizes=sizes),
+        in_specs=[anywhere, inside],
+        out_specs=[anywhere, inside],
+        out_shape=[jax.ShapeDtypeStruct(x.shape, x.dtype), jax.ShapeDtypeStruct(part.shape, f32)],
+        scratch_shapes=[
+            pltpu.VMEM((steps,) + part.shape, f32),
+            pltpu.VMEM((steps,) + part.shape, f32),
+            pltpu.SemaphoreType.DMA((1, count)),
+            pltpu.SemaphoreType.DMA((1, count)),
+            pltpu.SemaphoreType.DMA((1,)),
+            pltpu.SemaphoreType.DMA((steps,)),
+            pltpu.SemaphoreType.DMA((steps,)),
+        ],
+        compiler_params=pltpu.CompilerParams(collective_id=1, has_side_effects=True),
+        name="leave",
+    )(x, part)
+
+
+def permuted(x, me, count):
+    parts = [lax.dynamic_index_in_dim(x, me, 0, keepdims=False)]
+    for k in range(1, count):
+        mine = lax.dynamic_index_in_dim(x, lax.rem(me + k, count), 0, keepdims=False)
+        parts.append(lax.ppermute(mine, "head", [(d, (d + k) % count) for d in range(count)]))
+    out = x
+    for k in range(count):
+        out = lax.dynamic_update_index_in_dim(out, parts[k], lax.rem(me + count - k, count), 0)
+    return out
+
+
+def whole_slots(
+    block_input_rows,
+    document_starts,
+    counted_mask,
+    output_gradient,
+    first_norm_gain,
+    first_norm_bias,
+    query_key_value_weight,
+    query_down_weight,
+    query_up_weight,
+    value_down_weight,
+    value_up_weight,
+    attention_out_weight,
+    second_norm_gain,
+    second_norm_bias,
+    feed_input_weight,
+    feed_input_bias,
+    feed_output_weight,
+):
+    slots, local_len, width = block_input_rows.shape
+    sizes = (lax.axis_size("dp"), lax.axis_size("head"))
+    length = local_len * slots
+    size = width // H
+    rank = query_down_weight.shape[1]
+    me = lax.axis_index("head")
+
+    def row(v):
+        return v.astype(f32).reshape(1, -1)
+
+    starts = lax.dynamic_index_in_dim(document_starts, me, 0, keepdims=False).reshape(length, 1)
+    down = jnp.concatenate([query_down_weight, value_down_weight], 1)
+    blank = jnp.zeros_like(query_up_weight)
+    upq = jnp.concatenate([query_up_weight, blank], 0)
+    upv = jnp.concatenate([blank, value_up_weight], 0)
+    mask8 = jnp.broadcast_to(counted_mask.astype(f32)[:, None, :], (slots, 8, local_len))
+    gain_one = row(first_norm_gain)
+
+    x, masks = arrive(block_input_rows, mask8)
+    dy = permuted(output_gradient, me, slots)
+    mask = masks[:, 0, :].reshape(length, 1)
+    qkv, normed, low = project(x, gain_one, row(first_norm_bias), query_key_value_weight, down, upq, upv)
+    context, probs = attend(starts, qkv, size)
+    out, hidden_grad, context_grad, sums = feed(
+        x, dy, context, mask, attention_out_weight, row(second_norm_gain), row(second_norm_bias),
+        feed_input_weight, row(feed_input_bias), feed_output_weight,
+    )
+    output = permuted(out, me, slots)
+    dq, dk, dv = attend_back_slot(qkv, context_grad, context, probs, size)
+    grad, grads = project_back(
+        x, hidden_grad, dq, dk, dv, normed, low, gain_one, query_key_value_weight, down, upq, upv, sums
+    )
+    input_grad, total = leave(grad, grads, sizes)
+    count = jnp.maximum(total[4 * rank, 2], 1.0)
+    rms_values = jnp.stack(
+        [
+            jnp.sqrt(total[4 * rank, 0] / (count * width)),
+            jnp.sqrt(total[4 * rank, 1] / (2.0 * count * width)),
+        ]
+    )
+    return (
+        output,
+        input_grad,
+        total[0:rank].T,
+        total[2 * rank : 3 * rank],
+        total[rank : 2 * rank].T,
+        total[3 * rank : 4 * rank],
+        rms_values,
+    )
+
+
+def body(*args):
+    same = args[0].shape[0] == lax.axis_size("head")
+    return whole_slots(*args) if same else shards(*args)
+
+
 def solution(mesh):
     return jax.shard_map(
-        shards,
+        body,
         mesh=mesh,
         in_specs=(
             P("dp", "head", None),

time: 752 us -> 279 us (0.37); the launches traced: 740 us -> 278 us
  matrix products: 253 us -> 0 us
  waiting for transfers between devices: 250 us -> 0.02 us
  Pallas kernels: 0 us -> 228 us
  local copies, waits for them, and re-layouts: 116 us -> 36.5 us
  other arithmetic: 66.4 us -> 2.41 us
  starting transfers between devices: 36.3 us -> 8.17 us
  between operations: 17 us -> 3.02 us
    dot_general x75 -> x0, matrix products: 253 us -> none  [the longest x7 61.3 us: last_product(): lax.dot_general(left, right, (((1,), (1,)), ((), ())), preferred_element_...]
    pallas_call x0 -> x7, Pallas kernels: none -> 228 us  [the longest x1 55.3 us: feed(): pl.pallas_call(feed_kernel, grid=(blocks,), in_specs=[slab, slab, flat, p...]
    all_to_all x8 -> x0, waiting for transfers between devices: 136 us -> none  [the longest x1 25.8 us: shards(): lax.all_to_all(context_grad.reshape(local_shape), 'head', split_axis=2, c...]
    psum x1 -> x0, waiting for transfers between devices: 114 us -> none  [shards(): lax.psum((down_query, lifted_query, down_value, lifted_value, square_sums...]
    reshape x12 -> x2, local copies, waits for them, and re-layouts: 51.9 us -> 0.23 us  [whole_slots(): lax.dynamic_index_in_dim(document_starts, me, 0, keepdims=False)]
    all_to_all x8 -> x0, starting transfers between devices: 36.3 us -> none  [the longest x1 4.76 us: shards(): lax.all_to_all(as_sent(context_heads.reshape(merged_shape)), 'head', spli...]
    all_to_all x12 -> x0, local copies, waits for them, and re-layouts: 32.1 us -> none  [the longest x1 4.53 us: shards(): lax.all_to_all(key_rows.reshape(local_shape), 'head', split_axis=2, conca...]
    reduce_sum x14 -> x0, other arithmetic: 24 us -> none  [the longest x8 13 us: attend_slot(): row_total = jnp.sum(exponent, axis=-1, keepdims=True)]
  transfers between devices with their start and end apart: 9 -> 6, of which waited for: 9 -> 0; matrix products, arithmetic and copies ran while one was open for 10% -> 5% of each run, Pallas kernels for 0% -> 62%
where the time goes in v1:
time: 279 us; the launch traced here: 278 us
  Pallas kernels  228 us (82%)
  local copies, waits for them, and re-layouts  36.5 us (13%)
  starting transfers between devices  8.17 us (3%)
  between operations  3.02 us (1%)
    pallas_call x1, Pallas kernels, feed(): pl.pallas_call(feed_kernel, grid=(blocks,), in_specs=[slab, slab, flat, p...  55.3 us
    pallas_call x1, Pallas kernels, leave(): pl.pallas_call(functools.partial(leave_kernel, sizes=sizes), in_specs=[an...  45 us
    pallas_call x1, Pallas kernels, arrive(): pl.pallas_call(arrive_kernel, in_specs=[anywhere] * 2, out_specs=[anywher...  43.8 us
    pallas_call x1, Pallas kernels, attend_back_slot(): pl.pallas_call(functools.partial(attend_back_kernel, size=size, strip=32)...  31.8 us
    pallas_call x1, Pallas kernels, attend(): pl.pallas_call(functools.partial(attend_kernel, size=size, strip=32), gri...  24.5 us
    unnamed x54, local copies, waits for them, and re-layouts  18 us
    pallas_call x1, Pallas kernels, project_back(): pl.pallas_call(qkv_back_kernel, grid=(blocks,), in_specs=[slab, flat, fla...  14.1 us
    pallas_call x1, Pallas kernels, project(): pl.pallas_call(qkv_kernel, grid=(blocks,), in_specs=[pl.BlockSpec((1, til...  13.1 us
  transfers between devices with their start and end apart: 6, of which 0 were waited for; matrix products, arithmetic and copies ran while one was open for 5% of the time, Pallas kernels for 62%

profile of v1, /device:TPU:0, one launch (start us, length us, event | category | flops | bytes accessed | tf_op | source)
XLA Modules:
  0.0 277.9 jit_solution(17902998453719200459)
XLA Ops:
  0.6 1.6 copy.44
  2.4 1.2 dynamic-slice_bitcast_fusion.3
  4.0 2.5 collective-permute-start.1
  6.5 1.4 collective-permute-start.2
  9.2 43.8 %arrive.1 = (bf16[4,256,1024]{2,1,0:T(8,128)(2,1)}, f32[4,8,256]{2,1,0:T(8,128)}) custom-call(bf16[4,256,1024]{2,1,0:T(8,128)(2,1)} %x_ref.1, f32[4,8,256]{2,1,0:T(8,128)} %broadcast_in_dim.28.mask_ref), custom_call_target="tpu_custom_call" | custom-call | tf_op jit(solution)/shard_map/arrive/pallas_call | solution.py:769
  53.0 1.6 copy-done.4
  54.6 13.1 %project.1 = (bf16[1024,3072]{1,0:T(8,128)(2,1)S(1)}, bf16[1024,1024]{1,0:T(8,128)(2,1)S(1)}, bf16[1024,8]{1,0:T(8,128)(2,1)S(1)}) custom-call(bf16[4,256,1024]{2,1,0:T(8,128)(2,1)S(1)} %copy-done.4, f32[1,1024]{1,0:T(1,128)S(1)} %bitcast.38, f32[1,1024]{1,0:T(1,128)S(1)} %bitcast.40, bf16[1024,3072]{1,0:T(8,128)(2,1)} %w_ref.3, ...), custom_call_target="tpu_custom_call" | custom-call | flops 6442450944 | bytes 20971520 | tf_op jit(solution)/shard_map/project/pallas_call | solution.py:386
  67.7 1.4 copy-done.6
  69.1 2.6 copy-done.11
  71.7 24.5 %attend.1 = (bf16[1024,1024]{1,0:T(8,128)(2,1)S(1)}, bf16[16,1024,1024]{2,1,0:T(8,128)(2,1)}) custom-call(s32[1024,1]{1,0:T(8,128)S(1)} %copy.31.start_ref, bf16[1024,3072]{1,0:T(8,128)(2,1)} %copy-done.11, bf16[1024,3072]{1,0:T(8,128)(2,1)} %copy-done.11, bf16[1024,3072]{1,0:T(8,128)(2,1)} %copy-done.11), custom_call_target="tpu_custom_call" | custom-call | flops 20000000000 | bytes 41943040 | tf_op jit(solution)/shard_map/attend/pallas_call | solution.py:480
  96.2 1.4 copy-done.13
  101.2 1.1 bitcast_dynamic-update-slice_fusion.5
  102.3 1.1 bitcast_dynamic-update-slice_fusion.4
  103.4 1.1 bitcast_dynamic-update-slice_fusion.3.y_ref
  104.5 1.3 copy-done.14
  105.8 55.3 %feed.1 = (bf16[4,256,1024]{2,1,0:T(8,128)(2,1)}, bf16[1024,1024]{1,0:T(8,128)(2,1)}, bf16[1024,1024]{1,0:T(8,128)(2,1)}, f32[8,1024]{1,0:T(8,128)}) custom-call(bf16[4,256,1024]{2,1,0:T(8,128)(2,1)} %get-tuple-element.25.x_ref, bf16[4,256,1024]{2,1,0:T(8,128)(2,1)} %copy-done.14, bf16[1024,1024]{1,0:T(8,128)(2,1)} %copy-done.13, f32[1024,1]{1,0:T(8,128)} %copy.32.mask_ref, ...), custom_call_target="tpu_custom_call" | custom-call | flops 38654705664 | bytes 31457280 | tf_op jit(solution)/shard_map/feed/pallas_call | solution.py:647
  161.2 1.1 constant_dynamic-slice_fusion
  162.2 2.7 dynamic-slice_bitcast_fusion
  165.0 2.3 collective-permute-start.4
  167.3 1.4 collective-permute-start.5
  168.7 31.8 %attend_back.1 = (bf16[1024,1024]{1,0:T(8,128)(2,1)}, bf16[1024,1024]{1,0:T(8,128)(2,1)}, bf16[1024,1024]{1,0:T(8,128)(2,1)}) custom-call(bf16[1024,3072]{1,0:T(8,128)(2,1)} %copy-done.11, bf16[1024,3072]{1,0:T(8,128)(2,1)} %copy-done.11, bf16[1024,3072]{1,0:T(8,128)(2,1)} %copy-done.11, bf16[1024,1024]{1,0:T(8,128)(2,1)} %get-tuple-element.31.g_ref, ...), custom_call_target="tpu_custom_call" | custom-call | flops 30000001024 | bytes 47185920 | tf_op jit(solution)/shard_map/attend_back/pallas_call | solution.py:565
  200.6 1.6 copy-done.8
  202.2 1.6 copy-done.9
  203.8 1.6 copy-done.10
  205.4 14.1 %project_back.1 = (bf16[4,256,1024]{2,1,0:T(8,128)(2,1)S(1)}, f32[24,1024]{1,0:T(8,128)S(1)}) custom-call(bf16[4,256,1024]{2,1,0:T(8,128)(2,1)S(1)} %copy-done.5, bf16[1024,1024]{1,0:T(8,128)(2,1)S(1)} %copy-done.7, bf16[1024,1024]{1,0:T(8,128)(2,1)S(1)} %copy-done.8, bf16[1024,1024]{1,0:T(8,128)(2,1)S(1)} %copy-done.9, bf16[1024,1024]{1,0:T(8,128)(2,1)S(1)} %copy-done.10, ...), custom_call_target="tpu_custom_call" | custom-call | flops 6442450944 | bytes 20971520 | tf_op jit(solution)/shard_map/project_back/pallas_call | solution.py:708
  219.5 1.3 copy-done.2
  221.4 45.0 %leave.1 = (bf16[4,256,1024]{2,1,0:T(8,128)(2,1)}, f32[24,1024]{1,0:T(8,128)}) custom-call(bf16[4,256,1024]{2,1,0:T(8,128)(2,1)} %copy-done.2, f32[24,1024]{1,0:T(8,128)} %copy-done.3), custom_call_target="tpu_custom_call" | custom-call | tf_op jit(solution)/shard_map/leave/pallas_call | solution.py:823
  266.4 1.4 fusion.1
  269.9 1.5 fusion.2
  272.0 1.9 bitcast_dynamic-update-slice_fusion.2
  273.8 1.9 bitcast_dynamic-update-slice_fusion.1
  276.5 1.3 copy.45
  (69 shorter events, 7.3 us)
Async XLA Ops:
  0.6 7.4 %copy-start = (s32[4,1024]{1,0:T(4,128)S(1)}, s32[4,1024]{1,0:T(4,128)}, u32[]{:S(2)}) copy-start(s32[4,1024]{1,0:T(4,128)} %param.18) | copy-start | bytes 49156
  2.3 5.7 %copy-start.21 = (s32[4,256]{1,0:T(4,128)S(1)}, s32[4,256]{1,0:T(4,128)}, u32[]{:S(2)}) copy-start(s32[4,256]{1,0:T(4,128)} %param.19) | copy-start | bytes 12292
  2.3 5.9 %copy-start.22 = (bf16[1024]{0:T(1024)(128)(2,1)S(1)}, bf16[1024]{0:T(1024)(128)(2,1)}, u32[]{:S(2)}) copy-start(bf16[1024]{0:T(1024)(128)(2,1)} %param.21) | copy-start | bytes 6148
  2.3 5.9 %copy-start.23 = (bf16[1024]{0:T(1024)(128)(2,1)S(1)}, bf16[1024]{0:T(1024)(128)(2,1)}, u32[]{:S(2)}) copy-start(bf16[1024]{0:T(1024)(128)(2,1)} %param.22) | copy-start | bytes 6148
  2.3 5.9 %copy-start.19 = (bf16[1024,4]{0,1:T(4,128)(2,1)S(1)}, bf16[1024,4]{0,1:T(4,128)(2,1)}, u32[]{:S(2)}) copy-start(bf16[1024,4]{0,1:T(4,128)(2,1)} %param.26) | copy-start | bytes 24580
  2.3 5.9 %copy-start.20 = (bf16[1024,4]{0,1:T(4,128)(2,1)S(1)}, bf16[1024,4]{0,1:T(4,128)(2,1)}, u32[]{:S(2)}) copy-start(bf16[1024,4]{0,1:T(4,128)(2,1)} %param.24) | copy-start | bytes 24580
  2.4 6.1 %copy-start.16 = (bf16[4,1024]{1,0:T(4,128)(2,1)S(1)}, bf16[4,1024]{1,0:T(4,128)(2,1)}, u32[]{:S(2)}) copy-start(bf16[4,1024]{1,0:T(4,128)(2,1)} %param.25) | copy-start | bytes 24580
  2.4 6.1 %copy-start.17 = (bf16[4,1024]{1,0:T(4,128)(2,1)S(1)}, bf16[4,1024]{1,0:T(4,128)(2,1)}, u32[]{:S(2)}) copy-start(bf16[4,1024]{1,0:T(4,128)(2,1)} %param.27) | copy-start | bytes 24580
  3.6 97.6 %collective-permute-start = (bf16[256,1024]{1,0:T(8,128)(2,1)}, bf16[256,1024]{1,0:T(8,128)(2,1)}, u32[]{:S(2)}, u32[]{:S(2)}) collective-permute-start(bf16[256,1024]{1,0:T(8,128)(2,1)} %get-tuple-element.48), channel_id=1, source_target_pairs={{0,1},{1,2},{2,3},{3,0},{4,5},{5,6},{6,7},{7,4},{8,9},{9,10},{10,1... | collective-permute-start | bytes 1572872 | tf_op jit(solution)/shard_map/ppermute | solution.py:846
  4.0 98.3 %collective-permute-start.1 = (bf16[256,1024]{1,0:T(8,128)(2,1)}, bf16[256,1024]{1,0:T(8,128)(2,1)}, u32[]{:S(2)}, u32[]{:S(2)}) collective-permute-start(bf16[256,1024]{1,0:T(8,128)(2,1)} %get-tuple-element.50), channel_id=1, source_target_pairs={{0,2},{1,3},{2,0},{3,1},{4,6},{5,7},{6,4},{7,5},{8,10},{9,11},{10,... | collective-permute-start | bytes 1572872 | tf_op jit(solution)/shard_map/ppermute | solution.py:846
  6.5 96.9 %collective-permute-start.2 = (bf16[256,1024]{1,0:T(8,128)(2,1)}, bf16[256,1024]{1,0:T(8,128)(2,1)}, u32[]{:S(2)}, u32[]{:S(2)}) collective-permute-start(bf16[256,1024]{1,0:T(8,128)(2,1)} %get-tuple-element.47), channel_id=1, source_target_pairs={{0,3},{1,0},{2,1},{3,2},{4,7},{5,4},{6,5},{7,6},{8,11},{9,8},{10,9... | collective-permute-start | bytes 1572872 | tf_op jit(solution)/shard_map/ppermute | solution.py:846
  53.0 1.6 copy-start.4
  67.7 1.4 copy-start.6
  69.1 2.6 copy-start.11
  71.7 27.7 %copy-start.24 = (bf16[1024]{0:T(1024)(128)(2,1)S(1)}, bf16[1024]{0:T(1024)(128)(2,1)}, u32[]{:S(2)}) copy-start(bf16[1024]{0:T(1024)(128)(2,1)} %param.29) | copy-start | bytes 6148
  71.7 28.3 %copy-start.25 = (bf16[1024]{0:T(1024)(128)(2,1)S(1)}, bf16[1024]{0:T(1024)(128)(2,1)}, u32[]{:S(2)}) copy-start(bf16[1024]{0:T(1024)(128)(2,1)} %param.30) | copy-start | bytes 6148
  71.7 28.9 %copy-start.18 = (bf16[4096]{0:T(1024)(128)(2,1)S(1)}, bf16[4096]{0:T(1024)(128)(2,1)}, u32[]{:S(2)}) copy-start(bf16[4096]{0:T(1024)(128)(2,1)} %param.32) | copy-start | bytes 24580
  96.2 1.4 copy-start.13
  104.5 1.3 copy-start.14
  165.0 107.0 %collective-permute-start.3 = (bf16[256,1024]{1,0:T(8,128)(2,1)}, bf16[256,1024]{1,0:T(8,128)(2,1)}, u32[]{:S(2)}, u32[]{:S(2)}) collective-permute-start(bf16[256,1024]{1,0:T(8,128)(2,1)} %get-tuple-element.45), channel_id=1, source_target_pairs={{0,1},{1,2},{2,3},{3,0},{4,5},{5,6},{6,7},{7,4},{8,9},{9,10},{10,1... | collective-permute-start | bytes 1572872 | tf_op jit(solution)/shard_map/ppermute | solution.py:846
  165.0 108.9 %collective-permute-start.4 = (bf16[256,1024]{1,0:T(8,128)(2,1)}, bf16[256,1024]{1,0:T(8,128)(2,1)}, u32[]{:S(2)}, u32[]{:S(2)}) collective-permute-start(bf16[256,1024]{1,0:T(8,128)(2,1)} %get-tuple-element.44), channel_id=1, source_target_pairs={{0,2},{1,3},{2,0},{3,1},{4,6},{5,7},{6,4},{7,5},{8,10},{9,11},{10,... | collective-permute-start | bytes 1572872 | tf_op jit(solution)/shard_map/ppermute | solution.py:846
  167.3 108.4 %collective-permute-start.5 = (bf16[256,1024]{1,0:T(8,128)(2,1)}, bf16[256,1024]{1,0:T(8,128)(2,1)S(1)}, u32[]{:S(2)}, u32[]{:S(2)}) collective-permute-start(bf16[256,1024]{1,0:T(8,128)(2,1)} %get-tuple-element.43), channel_id=1, source_target_pairs={{0,3},{1,0},{2,1},{3,2},{4,7},{5,4},{6,5},{7,6},{8,11},{9,8},{10,9... | collective-permute-start | bytes 1572872 | tf_op jit(solution)/shard_map/ppermute | solution.py:846
  168.7 31.8 %copy-start.5 = (bf16[4,256,1024]{2,1,0:T(8,128)(2,1)S(1)}, bf16[4,256,1024]{2,1,0:T(8,128)(2,1)}, u32[]{:S(2)}) copy-start(bf16[4,256,1024]{2,1,0:T(8,128)(2,1)} %get-tuple-element.25.x_ref) | copy-start | bytes 6291460
  168.7 31.8 %copy-start.7 = (bf16[1024,1024]{1,0:T(8,128)(2,1)S(1)}, bf16[1024,1024]{1,0:T(8,128)(2,1)}, u32[]{:S(2)}) copy-start(bf16[1024,1024]{1,0:T(8,128)(2,1)} %get-tuple-element.30.hg_ref) | copy-start | bytes 6291460
  168.7 31.9 %copy-start.12 = (f32[8,1024]{1,0:T(8,128)S(1)}, f32[8,1024]{1,0:T(8,128)}, u32[]{:S(2)}) copy-start(f32[8,1024]{1,0:T(8,128)} %get-tuple-element.38.sums_ref) | copy-start | bytes 98308
  200.6 1.6 copy-start.8
  202.2 1.6 copy-start.9
  203.8 1.6 copy-start.10
  219.5 1.3 copy-start.2
  220.8 0.6 copy-start.3
  266.4 10.1 %copy-start.15 = (bf16[4,256,1024]{2,1,0:T(8,128)(2,1)S(1)}, bf16[4,256,1024]{2,1,0:T(8,128)(2,1)}, u32[]{:S(2)}) copy-start(bf16[4,256,1024]{2,1,0:T(8,128)(2,1)} %get-tuple-element.66) | copy-start | bytes 6291460
  276.5 1.3 copy-start.1
